TPU v7x, 32 devices: a whole 2x2x4 slice. The times are simulated.
32 devices in a mesh: book: 2 (over y), seq: 4 (over x, core), sub: 4 (over z).
Axes of the slice: x: 2, y: 2, z: 4, core: 2. Of those that a mesh axis runs over, the one named last changes fastest.
Arguments:
- queries: bfloat16 [16384, 2048], P(('book', 'seq'), 'sub'), parts along dimension 0, may hold values from -4 to 1920
- keys: bfloat16 [16384, 2048], P(('book', 'seq'), 'sub'), parts along dimension 0, may hold values from -6 to 4
- values: bfloat16 [16384, 2048], P(('book', 'seq'), 'sub'), parts along dimension 0, may hold values from -6 to 6
- decay: float32 [8, 8], P('book', 'sub'), parts along dimension 0, may hold values from 0.05 to 1
- gate: float32 [8], P('sub'), may hold values from -0.5 to 3
- summary: bfloat16 [512, 2048], P(('book', 'seq')), parts along dimension 0, may hold values from -6 to 6
- wq_sum: bfloat16 [2048, 2048], P(None, 'sub'), may hold values from -0.25 to 0.25
- wo_sum: bfloat16 [2048, 2048], P('sub'), may hold values from -0.125 to 0.125
Outputs:
- attended: bfloat16 [16384, 2048], P(('book', 'seq'), 'sub'), parts along dimension 0
- summarized: bfloat16 [512, 2048], P(('book', 'seq')), parts along dimension 0
There are 2 independent parts, one for each index of `book`. A program takes and returns all parts, laid end to end along the dimension named above; an argument that names none is the same for every part. Nothing has to cross between parts.
All inputs are finite; a program needn't handle non-finite values.
Results may differ from a plain program's by a relative error of at most 0.019.
Values may be sent and summed in bfloat16 or wider, within the bound.
A program may use at most 128 MiB of HBM per device.

v0:
```python
import jax
import jax.numpy as jnp
from jax import lax
from jax.sharding import PartitionSpec as P

SEG = 2048
STEPS = 4


top_precision = lax.Precision.HIGHEST


def carried_in(value, axis, join, neutral):
    count, mine = (lax.axis_size(axis), lax.axis_index(axis))
    pieces = jax.tree.map(lambda part: lax.all_gather(part, axis), value)
    so_far = jax.tree.map(
        lambda part, zero: jnp.full_like(part, 0) + jnp.asarray(zero, part.dtype), value, neutral
    )

    def step(position, so_far):
        longer = join(so_far, jax.tree.map(lambda part: part[position], pieces))
        return jax.tree.map(lambda new, old: jnp.where(position < mine, new, old), longer, so_far)

    return lax.fori_loop(0, count - 1, step, so_far)


def broadcast(x, axis, root):
    mine = lax.axis_index(axis) == root
    return lax.psum(jnp.where(mine, x, jnp.zeros_like(x)), axis)


def feature_map(inputs):
    return jax.nn.elu(inputs) + 1.0


def head_rms(inputs):
    return inputs * lax.rsqrt(jnp.mean(inputs * inputs, axis=-1, keepdims=True) + 1e-06)


def memory_read(lifted, memory, normalizer):
    numerator = jnp.einsum("qhd,hde->qhe", lifted, memory, precision=top_precision)
    denominator = jnp.einsum("qhd,hd->qh", lifted, normalizer, precision=top_precision) + 1.0
    return numerator / denominator[..., None]


def segment_attention(q_part, k_part, v_part):
    length = q_part.shape[0]
    block_rows = min(512, length)
    score_scale = q_part.shape[2] ** (-0.5)
    columns = jnp.arange(length)
    pieces = []
    for first_row in range(0, length, block_rows):
        scores = (
            jnp.einsum(
                "qhd,khd->hqk",
                q_part[first_row : first_row + block_rows],
                k_part,
                preferred_element_type=jnp.float32,
            )
            * score_scale
        )
        rows_here = first_row + jnp.arange(block_rows)
        scores = jnp.where(columns[None, None, :] <= rows_here[None, :, None], scores, -jnp.inf)
        weights = jax.nn.softmax(scores, axis=-1).astype(jnp.bfloat16)
        pieces.append(
            jnp.einsum("hqk,khd->qhd", weights, v_part, preferred_element_type=jnp.float32)
        )
    return jnp.concatenate(pieces, axis=0)


def on_device(queries, keys, values, decay, gate, summary, wq_sum, wo_sum):
    head_count = gate.shape[0]
    head_width = queries.shape[1] // head_count
    seg_count = queries.shape[0] // SEG
    position = lax.axis_index("seq")
    devices = lax.axis_size("seq")
    q_seg = queries.reshape(seg_count, SEG, head_count, head_width)
    k_seg = keys.reshape(seg_count, SEG, head_count, head_width)
    v_seg = values.reshape(seg_count, SEG, head_count, head_width)
    lifted_keys = feature_map(k_seg.astype(jnp.float32))
    updates = jnp.einsum(
        "jqhd,jqhe->jhde", lifted_keys, v_seg.astype(jnp.float32), precision=top_precision
    )
    key_sums = jnp.sum(lifted_keys, axis=1)
    local_decay = lax.dynamic_slice_in_dim(decay, position * seg_count, seg_count, 0)
    empty_memory = jnp.zeros((head_count, head_width, head_width), jnp.float32)
    empty_norm = jnp.zeros((head_count, head_width), jnp.float32)

    def accumulate(running, inputs_now):
        seg_decay, update, key_total = inputs_now
        return (
            (
                seg_decay[:, None, None] * running[0] + update,
                seg_decay[:, None] * running[1] + key_total,
            ),
            None,
        )

    (own_memory, own_norm), _ = lax.scan(
        accumulate, (empty_memory, empty_norm), (local_decay, updates, key_sums)
    )
    own_decay = jnp.prod(local_decay, axis=0)

    def combine(earlier, later):
        return (
            earlier[0] * later[0],
            later[0][:, None, None] * earlier[1] + later[1],
            later[0][:, None] * earlier[2] + later[2],
        )

    identity = (jnp.ones((head_count,), jnp.float32), empty_memory, empty_norm)
    _, prior_memory, prior_norm = carried_in(
        (own_decay, own_memory, own_norm), "seq", combine, identity
    )
    ending_memory = own_decay[:, None, None] * prior_memory + own_memory
    ending_norm = own_decay[:, None] * prior_norm + own_norm
    final_memory, final_norm = (
        broadcast(ending_memory, "seq", devices - 1),
        broadcast(ending_norm, "seq", devices - 1),
    )
    blend_weight = jax.nn.sigmoid(gate)[None, :, None]

    def one_segment(running, inputs_now):
        memory, normalizer = running
        q_part, k_part, v_part, seg_decay, update, key_total = inputs_now
        recalled = memory_read(feature_map(q_part.astype(jnp.float32)), memory, normalizer)
        local_out = segment_attention(q_part, k_part, v_part)
        mixed = head_rms(blend_weight * recalled + (1.0 - blend_weight) * local_out).astype(
            jnp.bfloat16
        )
        return (
            (
                seg_decay[:, None, None] * memory + update,
                seg_decay[:, None] * normalizer + key_total,
            ),
            mixed,
        )

    _, attended = lax.scan(
        one_segment,
        (prior_memory, prior_norm),
        (q_seg, k_seg, v_seg, local_decay, updates, key_sums),
    )
    attended = attended.reshape(seg_count * SEG, head_count * head_width)
    summary_state = summary
    row_count = summary.shape[0]
    for decode_step in range(STEPS):
        lifted = feature_map(
            jnp.dot(summary_state, wq_sum, preferred_element_type=jnp.float32).reshape(
                row_count, head_count, head_width
            )
        )
        recalled = head_rms(memory_read(lifted, final_memory, final_norm)).astype(jnp.bfloat16)
        partial_out = jnp.dot(
            recalled.reshape(row_count, head_count * head_width),
            wo_sum,
            preferred_element_type=jnp.float32,
        )
        summed = lax.psum(partial_out.astype(jnp.bfloat16), "sub").astype(jnp.float32)
        summary_state = (summary_state.astype(jnp.float32) + summed).astype(jnp.bfloat16)
    return (attended, summary_state)


def solution(mesh):
    placed = (
        P(("book", "seq"), "sub"),
        P(("book", "seq"), "sub"),
        P(("book", "seq"), "sub"),
        P("book", "sub"),
        P("sub"),
        P(("book", "seq"), None),
        P(None, "sub"),
        P("sub", None),
    )
    return jax.shard_map(
        on_device,
        mesh=mesh,
        in_specs=placed,
        out_specs=(P(("book", "seq"), "sub"), P(("book", "seq"), None)),
        check_vma=False,
    )
```

profile of v0, /device:TPU:0, one launch (start us, length us, event | category | flops | bytes accessed | tf_op | source)
XLA Modules:
  0.0 366.3 jit_solution(7190378475324766708)
XLA Ops:
  8.3 7.9 %fusion.73 = f32[2,256,256]{2,1,0:T(8,128)} fusion(bf16[256,2,8,256]{3,2,1,0:T(8,128)(2,1)} %bitcast.224, bf16[256,2,8,256]{3,2,1,0:T(8,128)(2,1)} %bitcast.186, f32[2]{0:T(128)S(1)} %broadcast_multiply_fusion), kind=kOutput, calls=%fused_computation.95 | convolution fusion | flops 3226599424 | bytes 4718600 | tf_op jit(solution)/shard_map/jqhd,jqhe->jhde/dot_general | solution.py:81
  18.3 2.7 fusion.170
  21.0 2.5 convert_element_type.126
  23.5 3.6 fusion.17
  29.7 6.4 %fusion.46 = f32[2,512,2048]{2,1,0:T(8,128)} fusion(bf16[512,2,256]{0,2,1:T(8,128)(2,1)} %bitcast.197, bf16[256,2,8,256]{3,2,1,0:T(8,128)(2,1)} %bitcast.187), kind=kOutput, calls=%fused_computation.76 | convolution fusion | flops 1073741824 | bytes 11010048 | tf_op jit(solution)/shard_map/while/body/eval_jaxpr/qhd,khd->hqk/dot_general | solution.py:54
  39.8 6.4 %fusion.48 = f32[2,512,2048]{2,1,0:T(8,128)} fusion(bf16[512,2,256]{0,2,1:T(8,128)(2,1)} %bitcast.198, bf16[256,2,8,256]{3,2,1,0:T(8,128)(2,1)} %bitcast.188), kind=kOutput, calls=%fused_computation.78 | convolution fusion | flops 1073741824 | bytes 11010048 | tf_op jit(solution)/shard_map/while/body/eval_jaxpr/qhd,khd->hqk/dot_general | solution.py:54
  49.8 6.4 %fusion.50 = f32[2,512,2048]{2,1,0:T(8,128)} fusion(bf16[512,2,256]{0,2,1:T(8,128)(2,1)} %bitcast.199, bf16[256,2,8,256]{3,2,1,0:T(8,128)(2,1)} %bitcast.189), kind=kOutput, calls=%fused_computation.80 | convolution fusion | flops 1073741824 | bytes 11010048 | tf_op jit(solution)/shard_map/while/body/eval_jaxpr/qhd,khd->hqk/dot_general | solution.py:54
  58.9 6.4 %fusion.52 = f32[2,512,2048]{2,1,0:T(8,128)} fusion(bf16[512,2,256]{0,2,1:T(8,128)(2,1)} %bitcast.200, bf16[256,2,8,256]{3,2,1,0:T(8,128)(2,1)} %bitcast.190), kind=kOutput, calls=%fused_computation.82 | convolution fusion | flops 1073741824 | bytes 11010048 | tf_op jit(solution)/shard_map/while/body/eval_jaxpr/qhd,khd->hqk/dot_general | solution.py:54
  65.8 6.0 %all-gather.1 = f32[4,1,2]{2,1,0:T(1,128)} all-gather(f32[1,1,2]{2,1,0:T(1,128)S(1)} %bitcast.214), channel_id=1, replica_groups=mesh['book'=2,'seq'=4,'sub'=4] {'seq'}, dimensions={0}, use_global_device_ids=true | all-gather | bytes 40 | tf_op jit(solution)/shard_map/all_gather | solution.py:15
  71.9 5.6 %all_gather.14 = f32[4,2,256]{2,1,0:T(2,128)S(1)} all-gather(f32[1,2,256]{2,1,0:T(2,128)S(1)} %broadcast_add_fusion), channel_id=1, replica_groups=mesh['book'=2,'seq'=4,'sub'=4] {'seq'}, dimensions={0}, use_global_device_ids=true | all-gather | bytes 10240 | tf_op jit(solution)/shard_map/all_gather | solution.py:15
  77.5 13.3 %fusion.171 = (f32[2,512]{1,0:T(2,128)S(1)}, f32[2,512,2048]{2,1,0:T(8,128)}) fusion(f32[2,512,2048]{2,1,0:T(8,128)} %fusion.46, pred[512,2048]{1,0:T(8,128)(4,1)} %iota_compare_fusion), kind=kOutput, calls=%fused_computation.225 | output fusion | flops 12584959 | bytes 17829888 | tf_op jit(solution)/shard_map/while/body/eval_jaxpr/sub | solution.py:64
  90.7 6.5 %fusion.61 = f32[512,2,256]{0,2,1:T(8,128)} fusion(f32[2,512,2048]{2,1,0:T(8,128)} %get-tuple-element.252, f32[2,512]{1,0:T(2,128)S(1)} %get-tuple-element.251, bf16[256,2,8,256]{3,2,1,0:T(8,128)(2,1)} %bitcast.225), kind=kOutput, calls=%fused_computation.91 | convolution fusion | flops 1077936128 | bytes 11538432 | tf_op jit(solution)/shard_map/while/body/eval_jaxpr/hqk,khd->qhd/dot_general | solution.py:66
  97.2 8.6 %fusion.172 = (f32[2,512]{1,0:T(2,128)S(1)}, f32[2,512,2048]{2,1,0:T(8,128)}) fusion(f32[2,512,2048]{2,1,0:T(8,128)S(1)} %bitcast.193, pred[512,2048]{1,0:T(8,128)(4,1)} %iota_compare_fusion.1), kind=kOutput, calls=%fused_computation.226 | output fusion | flops 12584959 | bytes 17829888 | tf_op jit(solution)/shard_map/while/body/eval_jaxpr/sub | solution.py:64
  105.8 6.5 %fusion.64 = f32[512,2,256]{0,2,1:T(8,128)} fusion(f32[2,512,2048]{2,1,0:T(8,128)} %get-tuple-element.254, f32[2,512]{1,0:T(2,128)S(1)} %get-tuple-element.253, bf16[256,2,8,256]{3,2,1,0:T(8,128)(2,1)} %bitcast.226), kind=kOutput, calls=%fused_computation.92 | convolution fusion | flops 1077936128 | bytes 11538432 | tf_op jit(solution)/shard_map/while/body/eval_jaxpr/hqk,khd->qhd/dot_general | solution.py:66
  112.4 13.0 %fusion.173 = (f32[2,512]{1,0:T(2,128)S(1)}, f32[2,512,2048]{2,1,0:T(8,128)}) fusion(f32[2,512,2048]{2,1,0:T(8,128)} %fusion.50, pred[512,2048]{1,0:T(8,128)(4,1)S(1)} %copy-done.6), kind=kOutput, calls=%fused_computation.227 | output fusion | flops 12584959 | bytes 17829888 | tf_op jit(solution)/shard_map/while/body/eval_jaxpr/sub | solution.py:64
  125.8 12.7 %fusion.174 = (f32[2,512]{1,0:T(2,128)S(1)}, f32[2,512,2048]{2,1,0:T(8,128)}) fusion(f32[2,512,2048]{2,1,0:T(8,128)} %fusion.52, pred[512,2048]{1,0:T(8,128)(4,1)S(1)} %copy-done.5), kind=kOutput, calls=%fused_computation.228 | output fusion | flops 12584959 | bytes 17829888 | tf_op jit(solution)/shard_map/while/body/eval_jaxpr/sub | solution.py:64
  138.6 6.0 %fusion.67 = f32[512,2,256]{0,2,1:T(8,128)} fusion(f32[2,512,2048]{2,1,0:T(8,128)} %get-tuple-element.256, f32[2,512]{1,0:T(2,128)S(1)} %get-tuple-element.255, bf16[256,2,8,256]{3,2,1,0:T(8,128)(2,1)S(1)} %bitcast.227), kind=kOutput, calls=%fused_computation.93 | convolution fusion | flops 1077936128 | bytes 11538432 | tf_op jit(solution)/shard_map/while/body/eval_jaxpr/hqk,khd->qhd/dot_general | solution.py:66
  144.6 2.5 fusion.70
  147.1 5.9 %while.10 = (s32[]{:T(128)}, f32[2,256,256]{2,1,0:T(8,128)S(1)}, f32[2,256]{1,0:T(2,128)S(1)}, s32[]{:T(128)}, f32[4,2]{1,0:T(4,128)}, /*index=5*/f32[4,2,256,25...) while((s32[]{:T(128)}, f32[2,256,256]{2,1,0:T(8,128)S(1)}, f32[2,256]{1,0:T(2,128)S(1)}, ...), condition=%wide.region_2.3_spmd.clone, body=%wide.region_1.2_spmd.clone.sunk | while | flops 526340 | bytes 1579175 | solution.py:24
  153.8 7.3 %psum.43 = f32[2,256]{1,0:T(2,128)S(1)} all-reduce(f32[2,256]{1,0:T(2,128)S(1)} %add_select_fusion.1), channel_id=1, replica_groups=mesh['book'=2,'seq'=4,'sub'=4] {'seq'}, use_global_device_ids=true, to_apply=%region_13.14 | all-reduce | flops 512 | bytes 4096 | tf_op jit(solution)/shard_map/psum | solution.py:29
  163.2 7.0 %fusion.38 = f32[2,1,2048]{2,1,0:T(1,128)S(1)} fusion(f32[256,2,8,256]{3,2,1,0:T(8,128)} %bitcast.194, f32[2,256,1]{1,0,2:T(2,128)S(1)} %bitcast.213), kind=kOutput, calls=%fused_computation.66 | convolution fusion | flops 16777216 | bytes 4212736 | tf_op jit(solution)/shard_map/while/body/eval_jaxpr/qhd,hd->qh/dot_general | solution.py:42
  170.4 26.0 %all-reduce.6.cloned.1.call-done = f32[2,256,256]{2,1,0:T(8,128)} async-done(((f32[2,256,256]{2,1,0:T(8,128)}), f32[2,256,256]{2,1,0:T(8,128)}) %all-reduce.6.cloned.1.call-update) | async-done | bytes 524304 | tf_op jit(solution)/shard_map/psum | solution.py:29
  199.5 35.4 %all-reduce.8.cloned.1.call-done = bf16[64,2048]{1,0:T(8,128)(2,1)} async-done(((bf16[64,2048]{1,0:T(8,128)(2,1)}), bf16[64,2048]{1,0:T(8,128)(2,1)}) %all-reduce.8.cloned.1.call-update) | async-done | bytes 262160 | tf_op jit(solution)/shard_map/psum | solution.py:159
  234.9 2.1 fusion.100
  240.5 17.1 %multiply_reduce_fusion = (f32[2048,2]{0,1:T(2,128)S(1)}, f32[2048,2,256]{0,2,1:T(8,128)}) fusion(f32[512,2,256]{0,2,1:T(8,128)} %fusion.61, f32[512,2,256]{0,2,1:T(8,128)} %fusion.64, f32[512,2,256]{0,2,1:T(8,128)} %fusion.67, f32[512,2,256]{0,2,1:T(8,128)} %fusion.70, f32[2]{0:T(128)S(1)} %copy-done.13, f32[2048,2]{0,1:T(2,128)S(1)} %fusion.134, ...), kind=kOutput, calls=%fused_computation.45 | convolution fusion | flops 3234852864 | bytes 13139984 | tf_op jit(solution)/shard_map/while/body/eval_jaxpr/qhd,hde->qhe/dot_general | solution.py:41
  257.6 17.8 %all-reduce.10.cloned.1.call-done = bf16[64,2048]{1,0:T(8,128)(2,1)} async-done(((bf16[64,2048]{1,0:T(8,128)(2,1)}), bf16[64,2048]{1,0:T(8,128)(2,1)}) %all-reduce.10.cloned.1.call-update) | async-done | bytes 262160 | tf_op jit(solution)/shard_map/psum | solution.py:159
  276.5 2.1 fusion.176
  281.8 35.2 %all-reduce.12.cloned.1.call-done = bf16[64,2048]{1,0:T(8,128)(2,1)} async-done(((bf16[64,2048]{1,0:T(8,128)(2,1)}), bf16[64,2048]{1,0:T(8,128)(2,1)}) %all-reduce.12.cloned.1.call-update) | async-done | bytes 262160 | tf_op jit(solution)/shard_map/psum | solution.py:159
  317.0 2.1 fusion.101
  322.4 4.1 %multiply_convert_fusion = bf16[2048,2,256]{0,2,1:T(8,128)(2,1)} fusion(f32[2048,2,256]{0,2,1:T(8,128)} %get-tuple-element.260, f32[2048,2]{0,1:T(2,128)S(1)} %add_rsqrt_fusion), kind=kLoop, calls=%fused_computation.44 | loop fusion | flops 2097152 | bytes 6307840 | tf_op jit(solution)/shard_map/while/body/eval_jaxpr/convert_element_type | solution.py:128
  326.4 3.9 %copy.135 = bf16[2048,512]{1,0:T(8,128)(2,1)} copy(bf16[2048,512]{0,1:T(8,128)(2,1)} %bitcast.191) | data formatting | bytes 4194304
  330.3 27.2 %all-reduce.14.cloned.1.call-done = bf16[64,2048]{1,0:T(8,128)(2,1)} async-done(((bf16[64,2048]{1,0:T(8,128)(2,1)}), bf16[64,2048]{1,0:T(8,128)(2,1)}) %all-reduce.14.cloned.1.call-update) | async-done | bytes 262160 | tf_op jit(solution)/shard_map/psum | solution.py:159
  (113 shorter events, 41.6 us)
Async XLA Ops:
  7.2 191.0 %copy-start = (bf16[512,2048]{1,0:T(8,128)(2,1)S(1)}, bf16[512,2048]{1,0:T(8,128)(2,1)}, u32[]{:S(2)}) copy-start(bf16[512,2048]{1,0:T(8,128)(2,1)} %param.17) | copy-start | bytes 6291460
  7.2 140.0 %all-gather.4.cloned.1.call-start = ((), (), s32[]{:S(2)}) async-start(), calls=%async_computation.5 | async-start | bytes 2621440 | tf_op jit(solution)/shard_map/all_gather | solution.py:15
  8.2 57.6 %copy-start.9 = (f32[2]{0:T(128)}, f32[2]{0:T(128)S(1)}, u32[]{:S(2)}) copy-start(f32[2]{0:T(128)S(1)} %dynamic-slice_reduce_fusion) | copy-start | bytes 28
  8.2 63.6 %copy-start.10 = (f32[2]{0:T(128)}, f32[2]{0:T(128)S(1)}, u32[]{:S(2)}) copy-start(f32[2]{0:T(128)S(1)} %broadcast_multiply_fusion) | copy-start | bytes 28
  16.2 180.3 %all-reduce.6.cloned.1.call-start = ((), (), s32[]{:S(2)}) async-start(), calls=%async_computation | async-start | bytes 1048576 | tf_op jit(solution)/shard_map/psum | solution.py:29
  16.7 4.2 %copy-start.2 = (bf16[2048,512]{1,0:T(8,128)(2,1)S(1)}, bf16[2048,512]{1,0:T(8,128)(2,1)}, u32[]{:S(2)}) copy-start(bf16[2048,512]{1,0:T(8,128)(2,1)} %param.10) | copy-start | bytes 6291460
  58.9 6.4 %copy-start.12 = (f32[2]{0:T(128)S(1)}, f32[2]{0:T(128)}, u32[]{:S(2)}) copy-start(f32[2]{0:T(128)} %param.14) | copy-start | bytes 28
  77.5 19.8 %slice-start = ((s8[8388608]{0:T(1024)(128)(4,1)}), s8[4194304]{0:T(1024)(128)(4,1)S(1)}, s32[]{:S(2)}) async-start(s8[8388608]{0:T(1024)(128)(4,1)} %bitcast.192), calls=%async_computation.6 | async-start | bytes 8388608
  90.7 6.5 %slice-start.1 = ((s8[8388608]{0:T(1024)(128)(4,1)}), s8[4194304]{0:T(1024)(128)(4,1)S(1)}, s32[]{:S(2)}) async-start(s8[8388608]{0:T(1024)(128)(4,1)} %bitcast.192), calls=%async_computation.7 | async-start | bytes 8388608
  105.8 6.5 %copy-start.6 = (pred[512,2048]{1,0:T(8,128)(4,1)S(1)}, pred[512,2048]{1,0:T(8,128)(4,1)}, u32[]{:S(2)}) copy-start(pred[512,2048]{1,0:T(8,128)(4,1)} %iota_compare_fusion.2) | copy-start | bytes 3145732
  112.3 13.0 %copy-start.1 = (bf16[2048,512]{1,0:T(8,128)(2,1)S(1)}, bf16[2048,512]{1,0:T(8,128)(2,1)}, u32[]{:S(2)}) copy-start(bf16[2048,512]{1,0:T(8,128)(2,1)} %param.16) | copy-start | bytes 6291460
  112.3 13.0 %copy-start.3 = (bf16[64,2048]{1,0:T(8,128)(2,1)S(1)}, bf16[64,2048]{1,0:T(8,128)(2,1)}, u32[]{:S(2)}) copy-start(bf16[64,2048]{1,0:T(8,128)(2,1)} %param.15) | copy-start | bytes 786436
  112.3 13.5 %copy-start.5 = (pred[512,2048]{1,0:T(8,128)(4,1)S(1)}, pred[512,2048]{1,0:T(8,128)(4,1)}, u32[]{:S(2)}) copy-start(pred[512,2048]{1,0:T(8,128)(4,1)} %iota_compare_fusion.3) | copy-start | bytes 3145732
  125.8 12.8 %copy-start.11 = (bf16[2048,512]{1,0:T(8,128)(2,1)S(1)}, bf16[2048,512]{1,0:T(8,128)(2,1)}, u32[]{:S(2)}) copy-start(bf16[2048,512]{1,0:T(8,128)(2,1)} %param.12) | copy-start | bytes 6291460
  138.6 6.0 %copy-start.15 = (f32[2,512,2048]{2,1,0:T(8,128)S(1)}, f32[2,512,2048]{2,1,0:T(8,128)}, u32[]{:S(2)}) copy-start(f32[2,512,2048]{2,1,0:T(8,128)} %get-tuple-element.258) | copy-start | bytes 25165828
  147.1 14.0 %copy-start.4 = (f32[2,256,256]{2,1,0:T(8,128)S(1)}, f32[2,256,256]{2,1,0:T(8,128)}, u32[]{:S(2)}) copy-start(f32[2,256,256]{2,1,0:T(8,128)} %fusion.73) | copy-start | bytes 1572868
  162.8 72.1 %all-reduce.8.cloned.1.call-start = ((), (), s32[]{:S(2)}) async-start(), calls=%async_computation.1 | async-start | bytes 524288 | tf_op jit(solution)/shard_map/psum | solution.py:159
  199.4 41.1 %copy-start.13 = (f32[2]{0:T(128)S(1)}, f32[2]{0:T(128)}, u32[]{:S(2)}) copy-start(f32[2]{0:T(128)} %get-tuple-element.245) | copy-start | bytes 28
  199.4 41.1 %copy-start.14 = (f32[2]{0:T(128)S(1)}, f32[2]{0:T(128)}, u32[]{:S(2)}) copy-start(f32[2]{0:T(128)} %get-tuple-element.246) | copy-start | bytes 28
  199.4 76.0 %all-reduce.10.cloned.1.call-start = ((), (), s32[]{:S(2)}) async-start(), calls=%async_computation.2 | async-start | bytes 524288 | tf_op jit(solution)/shard_map/psum | solution.py:159
  240.2 76.8 %all-reduce.12.cloned.1.call-start = ((), (), s32[]{:S(2)}) async-start(), calls=%async_computation.3 | async-start | bytes 524288 | tf_op jit(solution)/shard_map/psum | solution.py:159
  240.5 35.0 %copy-start.7 = (bf16[64,2048]{1,0:T(8,128)(2,1)S(1)}, bf16[64,2048]{1,0:T(8,128)(2,1)}, u32[]{:S(2)}) copy-start(bf16[64,2048]{1,0:T(8,128)(2,1)} %all-reduce.8.cloned.1.call-done) | copy-start | bytes 786436
  281.8 75.8 %all-reduce.14.cloned.1.call-start = ((), (), s32[]{:S(2)}) async-start(), calls=%async_computation.4 | async-start | bytes 524288 | tf_op jit(solution)/shard_map/psum | solution.py:159
  322.3 35.2 %copy-start.8 = (bf16[64,2048]{1,0:T(8,128)(2,1)S(1)}, bf16[64,2048]{1,0:T(8,128)(2,1)}, u32[]{:S(2)}) copy-start(bf16[64,2048]{1,0:T(8,128)(2,1)} %all-reduce.12.cloned.1.call-done) | copy-start | bytes 786436
Sparse Core Ops, SparseCore 0:
  16.3 25.2 all-gather.3
  162.9 33.5 all-reduce.5
  199.5 35.3 all-reduce.7
  240.3 35.0 all-reduce.9
  281.9 35.0 all-reduce.11
  322.5 35.0 all-reduce.13
where the time goes:
time: 372 us; the launch traced here: 366 us
  waiting for transfers between devices  142 us (38%)
  matrix products  98.1 us (26%)
  other arithmetic  74.1 us (20%)
  blocking collectives  18.9 us (5%)
  local copies, waits for them, and re-layouts  17.6 us (5%)
  between operations  14.6 us (4%)
    psum x4, waiting for transfers between devices, on_device(): lax.psum(partial_out.astype(jnp.bfloat16), 'sub').astype(jnp.float32)  116 us
    sub x4, other arithmetic, segment_attention(): weights = jax.nn.softmax(scores, axis=-1).astype(jnp.bfloat16)  47.5 us
    psum x1, waiting for transfers between devices, broadcast(): return lax.psum(jnp.where(mine, x, jnp.zeros_like(x)), axis)  26 us
    dot_general x4, matrix products, segment_attention(): jnp.einsum('qhd,khd->hqk', q_part[first_row:first_row + block_rows], k_pa...  25.5 us
    dot_general x5, matrix products, memory_read(): jnp.einsum('qhd,hde->qhe', lifted, memory, precision=top_precision)  23.6 us
    dot_general x4, matrix products, segment_attention(): jnp.einsum('hqk,khd->qhd', weights, v_part, preferred_element_type=jnp.fl...  21.6 us
    all_gather x2, blocking collectives, carried_in(): pieces = jax.tree.map(lambda part: lax.all_gather(part, axis), value)  11.6 us
    unnamed x41, local copies, waits for them, and re-layouts  11.2 us
  transfers between devices with their start and end apart: 6, of which 5 were waited for; matrix products, arithmetic and copies ran while one was open for 41% of the time, Pallas kernels for 0%

commit v1 on v0

v1 whole, which is shorter than its diff:
```python
import functools

import jax
import jax.numpy as jnp
from jax import lax
from jax.experimental import pallas as pl
from jax.experimental.pallas import tpu as pltpu
from jax.sharding import PartitionSpec as P

STEPS = 4
DH = 256
BLOCK = 256
LOG2E = 1.4426950408889634
F32 = jnp.float32
BF16 = jnp.bfloat16


def phi(x):
    return jnp.where(x > 0, x + 1.0, jnp.exp(jnp.minimum(x, 0.0)))


def rms(x):
    return x * lax.rsqrt(jnp.mean(x * x, axis=-1, keepdims=True) + 1e-06)


def kernel(
    ns, nz, heads,
    decay_ref, gate_ref, summary_ref, q_hbm, k_hbm, v_hbm, wq_hbm, wo_hbm,
    out_ref, sum_ref,
    q_ref, k_ref, v_ref, wq_ref, wo_ref,
    local_ref, mem_out, mem_in, prior_out, prior, final, nrm,
    part, part_in, state,
    load_sem, mem_ss, mem_rs, fin_ss, fin_rs, pri_ss, pri_rs, nrm_ss, nrm_rs,
    rs_ss, rs_rs, ag_ss, ag_rs,
):
    tokens = q_ref.shape[0]
    width = heads * DH
    slice_rows = DH // ns
    cols = wo_ref.shape[1] // nz
    me_s = lax.axis_index("seq")
    me_z = lax.axis_index("sub")

    loads = [
        pltpu.make_async_copy(src, dst, load_sem.at[i])
        for i, (src, dst) in enumerate(
            ((k_hbm, k_ref), (v_hbm, v_ref), (q_hbm, q_ref), (wq_hbm, wq_ref), (wo_hbm, wo_ref))
        )
    ]
    for load in loads:
        load.start()

    barrier = pltpu.get_barrier_semaphore()
    for o in range(1, ns):
        pl.semaphore_signal(barrier, inc=1, device_id={"seq": lax.rem(me_s + o, ns)},
                            device_id_type=pl.DeviceIdType.MESH)
    for o in range(1, nz):
        pl.semaphore_signal(barrier, inc=1, device_id={"sub": lax.rem(me_z + o, nz)},
                            device_id_type=pl.DeviceIdType.MESH)
    pl.semaphore_wait(barrier, ns - 1 + nz - 1)

    def to(axis, target, src, dst, ss, rs):
        return pltpu.make_async_remote_copy(
            src_ref=src, dst_ref=dst, send_sem=ss, recv_sem=rs,
            device_id={axis: target}, device_id_type=pl.DeviceIdType.MESH)

    loads[0].wait()
    loads[1].wait()
    for h in range(heads):
        col = pl.ds(h * DH, DH)
        lifted = phi(k_ref[:, col].astype(F32))
        nrm[me_s, :, col] = jnp.broadcast_to(jnp.sum(lifted, axis=0, keepdims=True), (8, DH))
        update = lax.dot_general(lifted.astype(BF16), v_ref[:, col], (((0,), (0,)), ((), ())),
                                 preferred_element_type=F32).astype(BF16)
        mem_out[:, h] = update.reshape(ns, slice_rows, DH)

    mem_copies, nrm_copies = [], []
    for o in range(1, ns):
        target = lax.rem(me_s + o, ns)
        mem_copies.append(to("seq", target, mem_out.at[target], mem_in.at[me_s],
                             mem_ss.at[o - 1], mem_rs.at[o - 1]))
        nrm_copies.append(to("seq", target, nrm.at[me_s], nrm.at[me_s],
                             nrm_ss.at[o - 1], nrm_rs.at[o - 1]))
    for copy in mem_copies + nrm_copies:
        copy.start()
    mem_in[me_s] = mem_out[me_s]

    scale = DH ** (-0.5) * LOG2E

    def attend(block, h):
        rows = pl.ds(block * BLOCK, BLOCK)
        col = pl.ds(h * DH, DH)
        span = (block + 1) * BLOCK
        scores = lax.dot_general(q_ref[rows, col], k_ref[pl.ds(0, span), col],
                                 (((1,), (1,)), ((), ())), preferred_element_type=F32)
        at_row = lax.broadcasted_iota(jnp.int32, (BLOCK, BLOCK), 0)
        at_col = lax.broadcasted_iota(jnp.int32, (BLOCK, BLOCK), 1)
        last = jnp.where(at_col <= at_row, scores[:, span - BLOCK:], -jnp.inf)
        if block:
            scores = jnp.concatenate([scores[:, : span - BLOCK], last], axis=1)
        else:
            scores = last
        top = jnp.max(scores, axis=1, keepdims=True)
        weights = jnp.exp2((scores - top) * scale)
        total = jnp.sum(weights, axis=1, keepdims=True)
        mixed = jnp.dot(weights.astype(BF16), v_ref[pl.ds(0, span), col],
                        preferred_element_type=F32)
        local_ref[rows, col] = mixed / total

    def finish(block, h, prior_norm):
        rows = pl.ds(block * BLOCK, BLOCK)
        col = pl.ds(h * DH, DH)
        lifted = phi(q_ref[rows, col].astype(F32))
        below = jnp.sum(lifted * prior_norm[:, h * DH:(h + 1) * DH], axis=1, keepdims=True) + 1.0
        above = jnp.dot(lifted.astype(BF16), prior[:, h].reshape(DH, DH),
                        preferred_element_type=F32)
        blend = 1.0 / (1.0 + jnp.exp(-jnp.full((1, DH), gate_ref[h], F32)))
        mixed = blend * (above / below) + (1.0 - blend) * local_ref[rows, col]
        out_ref[rows, col] = rms(mixed).astype(BF16)

    blocks = tokens // BLOCK
    units = []
    for h in range(heads):
        for i in range((blocks + 1) // 2):
            units.append([(b, h) for b in sorted({blocks - 1 - i, i}, reverse=True)])
    phases = 2 + 2 * STEPS
    early = 3
    plan = [[] for _ in range(phases)]
    for i, unit in enumerate(units):
        at = i * 8 // len(units)
        plan[at] += [("attend", pair) for pair in unit]
        if at < early:
            plan[8 + (at == early - 1)] += [("finish", pair) for pair in unit]
        else:
            plan[at] += [("finish", pair) for pair in unit]

    ready = {}

    def work(phase):
        for what, (block, h) in plan[phase]:
            if what == "attend":
                attend(block, h)
            else:
                finish(block, h, ready["prior_norm"])

    loads[2].wait()
    work(0)

    for copy in mem_copies:
        copy.wait()
    for h in range(heads):
        running = jnp.zeros((slice_rows, DH), F32)
        for s in range(ns):
            prior_out[s, h] = running.astype(BF16)
            running = decay_ref[s, h] * running + mem_in[s, h].astype(F32)
        final[me_s, h] = running.astype(BF16)
    fin_copies, pri_copies = [], []
    for o in range(1, ns):
        target = lax.rem(me_s + o, ns)
        fin_copies.append(to("seq", target, final.at[me_s], final.at[me_s],
                             fin_ss.at[o - 1], fin_rs.at[o - 1]))
        pri_copies.append(to("seq", target, prior_out.at[target], prior.at[me_s],
                             pri_ss.at[o - 1], pri_rs.at[o - 1]))
    for copy in fin_copies + pri_copies:
        copy.start()
    prior[me_s] = prior_out[me_s]

    work(1)

    for copy in nrm_copies:
        copy.wait()
    prior_parts, final_parts = [], []
    for h in range(heads):
        running = jnp.zeros((1, DH), F32)
        before = running
        for s in range(ns):
            before = jnp.where(me_s == s, running, before)
            running = decay_ref[s, h] * running + nrm[s, 0:1, h * DH:(h + 1) * DH]
        prior_parts.append(before)
        final_parts.append(running)
    ready["prior_norm"] = jnp.concatenate(prior_parts, axis=1)

    for copy in fin_copies:
        copy.wait()

    for o in range(nz):
        source = lax.rem(me_z + nz - o, nz)
        state[o] = summary_ref[:, pl.ds(pl.multiple_of(source * cols, cols), cols)]
    loads[3].wait()
    loads[4].wait()
    for step in range(STEPS):
        lifted = None
        for o in range(nz):
            source = lax.rem(me_z + nz - o, nz)
            rows = pl.ds(pl.multiple_of(source * cols, cols), cols)
            term = jnp.dot(state[o], wq_ref[rows, :], preferred_element_type=F32)
            lifted = term if lifted is None else lifted + term
        lifted = phi(lifted)
        reads = []
        for h in range(heads):
            mine = lifted[:, h * DH:(h + 1) * DH]
            below = jnp.sum(mine * final_parts[h], axis=1, keepdims=True) + 1.0
            above = jnp.dot(mine.astype(BF16), final[:, h].reshape(DH, DH),
                            preferred_element_type=F32)
            reads.append(rms(above / below).astype(BF16))
        read = jnp.concatenate(reads, axis=1) if heads > 1 else reads[0]
        copies = []
        for o in range(1, nz):
            target = lax.rem(me_z + o, nz)
            there = pl.ds(pl.multiple_of(target * cols, cols), cols)
            part[o - 1] = jnp.dot(read, wo_ref[:, there], preferred_element_type=F32).astype(BF16)
            copy = to("sub", target, part.at[o - 1], part_in.at[o - 1],
                      rs_ss.at[o - 1], rs_rs.at[o - 1])
            copy.start()
            copies.append(copy)
        here = pl.ds(pl.multiple_of(me_z * cols, cols), cols)
        total = jnp.dot(read, wo_ref[:, here], preferred_element_type=F32)

        if step == 0:
            work(2)
            for copy in pri_copies:
                copy.wait()
        else:
            work(2 + 2 * step)

        for copy in copies:
            copy.wait()
        for o in range(1, nz):
            total = total + part_in[o - 1].astype(F32)
        state[0] = (state[0].astype(F32) + total).astype(BF16)
        copies = []
        for o in range(1, nz):
            target = lax.rem(me_z + o, nz)
            copy = to("sub", target, state.at[0], state.at[o], ag_ss.at[o - 1], ag_rs.at[o - 1])
            copy.start()
            copies.append(copy)
        work(3 + 2 * step)
        for copy in copies:
            copy.wait()
    for o in range(nz):
        source = lax.rem(me_z + nz - o, nz)
        sum_ref[:, pl.ds(pl.multiple_of(source * cols, cols), cols)] = state[o]


def on_device(queries, keys, values, decay, gate, summary, wq_sum, wo_sum):
    ns, nz = lax.axis_size("seq"), lax.axis_size("sub")
    heads = gate.shape[0]
    tokens, width = queries.shape
    rows, model = summary.shape
    cols = model // nz
    slice_rows = DH // ns
    whole = pl.BlockSpec(memory_space=pltpu.VMEM)
    scalars = pl.BlockSpec(memory_space=pltpu.SMEM)
    anywhere = pl.BlockSpec(memory_space=pl.ANY)
    sems = lambda count: pltpu.SemaphoreType.DMA((count,))
    return pl.pallas_call(
        functools.partial(kernel, ns, nz, heads),
        out_shape=(
            jax.ShapeDtypeStruct((tokens, width), BF16),
            jax.ShapeDtypeStruct((rows, model), BF16),
        ),
        in_specs=[scalars, scalars, whole] + [anywhere] * 5,
        out_specs=(whole, whole),
        scratch_shapes=[
            pltpu.VMEM((tokens, width), BF16),
            pltpu.VMEM((tokens, width), BF16),
            pltpu.VMEM((tokens, width), BF16),
            pltpu.VMEM((model, width), BF16),
            pltpu.VMEM((width, model), BF16),
            pltpu.VMEM((tokens, width), F32),
            pltpu.VMEM((ns, heads, slice_rows, DH), BF16),
            pltpu.VMEM((ns, heads, slice_rows, DH), BF16),
            pltpu.VMEM((ns, heads, slice_rows, DH), BF16),
            pltpu.VMEM((ns, heads, slice_rows, DH), BF16),
            pltpu.VMEM((ns, heads, slice_rows, DH), BF16),
            pltpu.VMEM((ns, 8, width), F32),
            pltpu.VMEM((nz - 1, rows, cols), BF16),
            pltpu.VMEM((nz - 1, rows, cols), BF16),
            pltpu.VMEM((nz, rows, cols), BF16),
            sems(5),
            sems(ns - 1), sems(ns - 1), sems(ns - 1), sems(ns - 1),
            sems(ns - 1), sems(ns - 1), sems(ns - 1), sems(ns - 1),
            sems(nz - 1), sems(nz - 1), sems(nz - 1), sems(nz - 1),
        ],
        compiler_params=pltpu.CompilerParams(
            collective_id=0, has_side_effects=True, vmem_limit_bytes=56 * 1024 * 1024
        ),
        cost_estimate=pl.CostEstimate(
            flops=7 * 10**9, bytes_accessed=12 * 2**20, transcendentals=6 * 10**6
        ),
    )(decay, gate, summary, queries, keys, values, wq_sum, wo_sum)


def solution(mesh):
    placed = (
        P(("book", "seq"), "sub"),
        P(("book", "seq"), "sub"),
        P(("book", "seq"), "sub"),
        P("book", "sub"),
        P("sub"),
        P(("book", "seq"), None),
        P(None, "sub"),
        P("sub", None),
    )
    return jax.shard_map(
        on_device,
        mesh=mesh,
        in_specs=placed,
        out_specs=(P(("book", "seq"), "sub"), P(("book", "seq"), None)),
        check_vma=False,
    )
```

time: 372 us -> 81.3 us (0.22); the launches traced: 366 us -> 81.1 us
  waiting for transfers between devices: 142 us -> 0 us
  matrix products: 98.1 us -> 0 us
  Pallas kernels: 0 us -> 75.3 us
  other arithmetic: 74.1 us -> 0 us
  blocking collectives: 18.9 us -> 0 us
  between operations: 14.6 us -> 0.65 us
  local copies, waits for them, and re-layouts: 17.6 us -> 5.13 us
    psum x5 -> x0, waiting for transfers between devices: 142 us -> none  [the longest x4 116 us: on_device(): lax.psum(partial_out.astype(jnp.bfloat16), 'sub').astype(jnp.float32)]
    dot_general x27 -> x0, matrix products: 98.1 us -> none  [the longest x4 25.5 us: segment_attention(): jnp.einsum('qhd,khd->hqk', q_part[first_row:first_row + block_rows], k_pa...]
    pallas_call x0 -> x1, Pallas kernels: none -> 75.3 us  [on_device(): pl.pallas_call(functools.partial(kernel, ns, nz, heads), out_shape=(jax.S...]
    sub x5 -> x0, other arithmetic: 48.1 us -> none  [the longest x4 47.5 us: segment_attention(): weights = jax.nn.softmax(scores, axis=-1).astype(jnp.bfloat16)]
    all_gather x2 -> x0, blocking collectives: 11.6 us -> none  [carried_in(): pieces = jax.tree.map(lambda part: lax.all_gather(part, axis), value)]
    convert_element_type x4 -> x0, other arithmetic: 9.37 us -> none  [the longest x1 4.06 us: one_segment(): head_rms(blend_weight * recalled + (1.0 - blend_weight) * local_out)]
    psum x1 -> x0, blocking collectives: 7.3 us -> none  [broadcast(): return lax.psum(jnp.where(mine, x, jnp.zeros_like(x)), axis)]
    le x4 -> x0, other arithmetic: 6.4 us -> none  [segment_attention(): columns[None, None, :] <= rows_here[None, :, None]]
  transfers between devices with their start and end apart: 6 -> 0, of which waited for: 5 -> 0; matrix products, arithmetic and copies ran while one was open for 41% -> 0% of each run, Pallas kernels for 0% -> 0%
where the time goes in v1:
time: 81.3 us; the launch traced here: 81.1 us
  Pallas kernels  75.3 us (93%)
  local copies, waits for them, and re-layouts  5.13 us (6%)
    pallas_call x1, Pallas kernels, on_device(): pl.pallas_call(functools.partial(kernel, ns, nz, heads), out_shape=(jax.S...  75.3 us
    unnamed x5, local copies, waits for them, and re-layouts  5.13 us

profile of v1, /device:TPU:0, one launch (start us, length us, event | category | flops | bytes accessed | tf_op | source)
XLA Modules:
  0.0 81.1 jit_solution(2333610543826815754)
XLA Ops:
  0.6 1.3 %copy.10.decay_ref = f32[4,2]{1,0:T(4,128)} copy(f32[4,2]{0,1:T(2,128)} %param.11) | data formatting | bytes 64 | tf_op args[3]
  2.0 75.3 %shard_map.95 = (bf16[2048,512]{1,0:T(8,128)(2,1)}, bf16[64,2048]{1,0:T(8,128)(2,1)}) custom-call(f32[4,2]{1,0:T(4,128)} %copy.10.decay_ref, f32[2]{0:T(128)} %gate_ref.1, bf16[64,2048]{1,0:T(8,128)(2,1)} %summary_ref.1, bf16[2048,512]{1,0:T(8,128)(2,1)} %q_hbm.1, bf16[2048,512]{1,0:T(8,128)(2,1)} %k_hbm.1, bf16[2048,512]{1,0:T(8,128)(2,1)} %v_hbm.1, ...), custom_call_target="tpu_custom_call" | custom-call | flops 7000000000 | bytes 12582912 | tf_op jit(solution)/shard_map/pallas_call | solution.py:255
  77.3 0.0 copy-start
  77.3 3.1 %copy.13 = bf16[2048,512]{1,0:T(8,128)(2,1)} copy(bf16[2048,512]{1,0:T(8,128)(2,1)} %get-tuple-element.4) | data formatting | bytes 4194304
  80.4 0.0 copy-done
  80.4 0.7 copy.14
Async XLA Ops:
  77.3 3.1 %copy-start = (bf16[64,2048]{1,0:T(8,128)(2,1)S(1)}, bf16[64,2048]{1,0:T(8,128)(2,1)}, u32[]{:S(2)}) copy-start(bf16[64,2048]{1,0:T(8,128)(2,1)} %get-tuple-element.5) | copy-start | bytes 786436
